TPU v7x, 128 devices: a whole 4x4x4 slice. The times are simulated.
128 devices in a mesh: seq: 16 (over x, y), head: 8 (over z, core).
Axes of the slice: x: 4, y: 4, z: 4, core: 2. Of those that a mesh axis runs over, the one named last changes fastest.
Arguments:
- lin_qk: float32 [32768, 1024], P('seq', 'head'), may hold values from -6 to 6
- lin_v: float32 [32768, 4096], P('seq', 'head'), may hold values from -64 to 64
- conv_qk: float32 [3, 1024], P(None, 'head'), may hold values from -3.5 to 3.5
- conv_v: float32 [3, 4096], P(None, 'head'), may hold values from -3.5 to 3.5
- swa_qkv: float32 [32768, 3, 4096], P('seq', None, 'head'), may hold values from -5.5 to 5.5
- head_gain: float32 [4096], P('head'), may hold values from 0.5 to 13.5
Outputs:
- mixed: float32 [32768, 4096], P('seq', 'head')
All inputs are finite; a program needn't handle non-finite values.
Results may differ from a plain program's by a relative error of at most 0.0003.
Values sent between devices are 32-bit elements; how exact they have to be, the bound alone decides.
A program may use at most 192 MiB of HBM per device.

v0:
```python
import functools
import math

import jax
import jax.numpy as jnp
from jax import lax
from jax.experimental import pallas as pl
from jax.experimental.pallas import tpu as pltpu
from jax.sharding import PartitionSpec as P

DK = 16
DV = 128
WIN = 64
C = 128
ROWS = 160
MESH = pl.DeviceIdType.MESH
F32 = jnp.float32
BF16 = jnp.bfloat16


def split(value):
    high = value.astype(BF16)
    low = (value - high.astype(F32)).astype(BF16)
    return high, low


def dot(left, right, dims=((1,), (0,))):
    return lax.dot_general(left, right, (dims, ((), ())), preferred_element_type=F32)


def fold(value):
    return value[:, :DV] + value[:, DV:]


def feature_rows(load, pair, linear, constant):
    base = load(0, DK)
    twice = base if pair == 1 else base * pair
    rows = [base * base]
    rows += [twice * load(shift, DK) for shift in range(1, DK // 2)]
    rows += [twice[: DK // 2] * load(DK // 2, DK // 2)]
    rows += [base if linear == 1 else base * linear]
    first = lax.broadcasted_iota(jnp.int32, (8, base.shape[1]), 0) == 0
    rows += [jnp.where(first, F32(constant), F32(0.0))]
    return jnp.concatenate(rows, axis=0)


def kernel(
    seqs, heads,
    qk_hbm, v_hbm, swa_hbm, wqk_ref, wv_ref, gain_ref,
    out_hbm, total_ref,
    xin, vin, qin, kin, xs, xt, us, sx, lin, win, ostage,
    mine, got, prefs, pref, sq, sqgot,
    in_sem, swa_sem, out_sem, hs_sem, hr_sem, s1, r1, s2, r2, s3, r3,
):
    tokens = xs.shape[0]
    local = vin.shape[0]
    chunks = tokens // C
    part = local * ROWS // seqs
    me = lax.axis_index("seq")
    my_head = lax.axis_index("head")

    barrier = pltpu.get_barrier_semaphore()
    for step in range(1, seqs):
        pl.semaphore_signal(barrier, inc=1, device_id={"seq": lax.rem(me + step, seqs)}, device_id_type=MESH)
    for step in range(1, heads):
        pl.semaphore_signal(barrier, inc=1, device_id={"head": lax.rem(my_head + step, heads)}, device_id_type=MESH)

    loads = [pltpu.make_async_copy(qk_hbm, xin.at[pl.ds(8, tokens)], in_sem.at[0])]
    for h in range(local):
        loads.append(pltpu.make_async_copy(
            v_hbm.at[:, pl.ds(h * DV, DV)], vin.at[h, pl.ds(8, tokens)], in_sem.at[1 + h]))
    for load in loads:
        load.start()
    swa_loads = []
    for h in range(local):
        columns = pl.ds(h * DV, DV)
        swa_loads.append(pltpu.make_async_copy(swa_hbm.at[0, :, columns], qin.at[h], swa_sem.at[h, 0]))
        for which in range(2):
            swa_loads.append(pltpu.make_async_copy(
                swa_hbm.at[1 + which, :, columns], kin.at[which, h, pl.ds(WIN, tokens)], swa_sem.at[h, 1 + which]))
    for load in swa_loads:
        load.start()

    pl.semaphore_wait(barrier, seqs - 1 + heads - 1)
    after = {"seq": lax.rem(me + 1, seqs)}

    def remote(source, target, send, receive, device):
        return pltpu.make_async_remote_copy(
            src_ref=source, dst_ref=target, send_sem=send, recv_sem=receive, device_id=device, device_id_type=MESH)

    tail = pl.ds(tokens - 8, 8)
    halos = [remote(qk_hbm.at[tail], xin.at[pl.ds(0, 8)], hs_sem.at[0], hr_sem.at[0], after)]
    for h in range(local):
        halos.append(remote(v_hbm.at[tail, pl.ds(h * DV, DV)], vin.at[h, pl.ds(0, 8)],
                            hs_sem.at[1 + h], hr_sem.at[1 + h], after))
    window_halos = []
    for h in range(local):
        for which in range(2):
            slot = 1 + local + 2 * h + which
            window_halos.append(remote(
                swa_hbm.at[1 + which, pl.ds(tokens - WIN, WIN), pl.ds(h * DV, DV)],
                kin.at[which, h, pl.ds(0, WIN)], hs_sem.at[slot], hr_sem.at[slot], after))
    for copy in halos + window_halos:
        copy.start()

    sx[0] = jnp.zeros(sx.shape[1:], F32)
    for load in loads:
        load.wait()

    def state_step(i, carry):
        c = lax.rem(i + 1, chunks)
        row = pl.multiple_of(c * C, C)

        @pl.when(i == chunks - 1)
        def _():
            for copy in halos:
                copy.wait_recv()
            keep = me > 0
            xin[pl.ds(0, 8)] = jnp.where(keep, xin[pl.ds(0, 8)], 0.0)
            for h in range(local):
                vin[h, pl.ds(0, 8)] = jnp.where(keep, vin[h, pl.ds(0, 8)], 0.0)

        x = wqk_ref[0:1] * xin[pl.ds(row + 6, C)]
        x = x + wqk_ref[1:2] * xin[pl.ds(row + 7, C)]
        x = x + wqk_ref[2:3] * xin[pl.ds(row + 8, C)]
        xs[pl.ds(row, C)] = x
        turned = x.T
        for h in range(local):
            for which in range(2):
                piece = turned[(2 * h + which) * DK:(2 * h + which + 1) * DK]
                xt[c, 2 * h + which, 0:DK] = piece
                xt[c, 2 * h + which, DK:2 * DK] = piece
        again = jnp.where(i < chunks - 1, 1.0, 0.0).astype(F32)
        for h in range(local):
            columns = slice(h * DV, (h + 1) * DV)
            u = wv_ref[0:1, columns] * vin[h, pl.ds(row + 6, C)]
            u = u + wv_ref[1:2, columns] * vin[h, pl.ds(row + 7, C)]
            u = u + wv_ref[2:3, columns] * vin[h, pl.ds(row + 8, C)]
            both = jnp.concatenate(split(u), axis=1)
            us[h, pl.ds(row, C)] = both
            phi = feature_rows(lambda start, size: xt[c, 2 * h + 1, start:start + size], 1, 1, 1.0)
            state = fold(dot(jnp.concatenate(split(phi), axis=1), jnp.concatenate([both, both], axis=0)))
            rows = slice(h * ROWS, (h + 1) * ROWS)
            sx[i + 1, rows] = sx[i, rows] * again + state
        return carry

    lax.fori_loop(0, chunks, state_step, 0)

    mine[...] = sx[chunks - 1] + sx[chunks]
    first = []
    for step in range(1, seqs):
        peer = lax.rem(me + step, seqs)
        rows = pl.ds(pl.multiple_of(peer * part, 8), part)
        first.append(remote(mine.at[rows], got.at[me], s1.at[step - 1], r1.at[step - 1], {"seq": peer}))
        first[-1].start()
    got[me] = mine[pl.ds(pl.multiple_of(me * part, 8), part)]

    lane = lax.broadcasted_iota(jnp.int32, (C, C), 1)
    sub = lax.broadcasted_iota(jnp.int32, (C, C), 0)
    query_lane = lax.rem(lane, 2 * DK) < DK
    causal = lane <= sub

    def local_step(c, carry):
        row = pl.multiple_of(c * C, C)
        x = xs[pl.ds(row, C)]
        left = jnp.concatenate(split(jnp.where(query_lane, x, pltpu.roll(x, DK, 1))), axis=1)
        for pair in range(local // 2):
            sides = []
            for h in (2 * pair, 2 * pair + 1):
                high, low = split(xt[c, 2 * h + 1, 0:DK])
                blank = jnp.zeros((DK, C), BF16)
                pieces = [blank] * (2 * 2 * local)
                pieces[2 * h] = high
                pieces[2 * h + 1] = low
                pieces[2 * local + 2 * h] = high
                sides.append(jnp.concatenate(pieces, axis=0))
            scores = dot(left, jnp.concatenate(sides, axis=1))
            for which in range(2):
                h = 2 * pair + which
                value = scores[:, which * C:(which + 1) * C] + 4.0
                value = jnp.where(causal, value * value + 16.0, 0.0)
                both = us[h, pl.ds(row, C)]
                lin[h, pl.ds(row, C)] = fold(
                    dot(jnp.concatenate(split(value), axis=1), jnp.concatenate([both, both], axis=0)))
        return carry

    lax.fori_loop(0, chunks, local_step, 0)

    for copy in first:
        copy.wait_recv()

    def prefix_step(d, carry):
        prefs[d] = carry
        return carry + got[d]

    lax.fori_loop(0, seqs, prefix_step, jnp.zeros((part, DV), F32))
    own_rows = pl.ds(pl.multiple_of(me * part, 8), part)
    second = []
    for step in range(1, seqs):
        peer = lax.rem(me + step, seqs)
        second.append(remote(prefs.at[peer], pref.at[own_rows], s2.at[step - 1], r2.at[step - 1], {"seq": peer}))
        second[-1].start()
    pref[own_rows] = prefs[me]

    for load in swa_loads:
        load.wait()
    for copy in window_halos:
        copy.wait_recv()
    key = lax.broadcasted_iota(jnp.int32, (WIN, 2 * WIN), 1)
    query = lax.broadcasted_iota(jnp.int32, (WIN, 2 * WIN), 0)
    scale = math.log2(math.e) / math.sqrt(DV)

    def window_step(c, carry):
        row = pl.multiple_of(c * C, C)
        lowest = jnp.where((c == 0) & (me == 0), WIN, 0)
        biases = []
        for b in range(C // WIN):
            low_key = jnp.maximum(query + 1, lowest) if b == 0 else query + 1
            biases.append(jnp.where((key >= low_key) & (key <= query + WIN), 0.0, -1e30).astype(F32))
        for h in range(local):
            q_both = jnp.concatenate(split(qin[h, pl.ds(row, C)] * scale), axis=1)
            k_high, k_low = split(kin[0, h, pl.ds(row, C + WIN)])
            k_high = jnp.concatenate([k_high, k_high], axis=1)
            k_low = jnp.concatenate([k_low, k_low], axis=1)
            v_both = jnp.concatenate(split(kin[1, h, pl.ds(row, C + WIN)]), axis=1)
            for b in range(C // WIN):
                at = slice(b * WIN, b * WIN + 2 * WIN)
                keys = jnp.concatenate([k_high[at], k_low[at]], axis=0)
                scores = fold(dot(q_both[b * WIN:(b + 1) * WIN], keys, ((1,), (1,)))) + biases[b]
                peak = jnp.max(scores, axis=1, keepdims=True)
                weights = jnp.exp2(scores - peak)
                norm = jnp.sum(weights, axis=1, keepdims=True)
                values = jnp.concatenate([v_both[at], v_both[at]], axis=0)
                mixed = fold(dot(jnp.concatenate(split(weights), axis=1), values))
                win[h, pl.ds(row + b * WIN, WIN)] = mixed / norm
        return carry

    lax.fori_loop(0, chunks, window_step, 0)

    for copy in second:
        copy.wait_recv()
    prefs_for = mine

    def carried_step(c, carry):
        row = pl.multiple_of(c * C, C)
        squares = jnp.zeros((C, DV), F32)
        later = jnp.where(c > 0, 1.0, 0.0).astype(F32)
        at = jnp.maximum(c - 1, 0)
        for h in range(local):
            phi_high, phi_low = split(
                feature_rows(lambda start, size: xt[c, 2 * h, start:start + size], 2.0, 8.0, 32.0))
            rows = slice(h * ROWS, (h + 1) * ROWS)
            state = sx[at, rows] + (pref[rows] + sx[chunks, rows] * later)
            both = jnp.concatenate(split(state), axis=1)
            earlier = fold(dot(phi_high, both, ((0,), (0,))) + dot(phi_low, both, ((0,), (0,))))
            mix = lin[h, pl.ds(row, C)] + earlier
            mean = jnp.sum(mix * mix, axis=1, keepdims=True) * (1.0 / DV)
            columns = slice(h * DV, (h + 1) * DV)
            value = mix * lax.rsqrt(mean + 1024.0e-6) * gain_ref[0:1, columns] + win[h, pl.ds(row, C)]
            ostage[pl.ds(row, C), columns] = value
            squares = squares + value * value
        sq[c] = jnp.sum(squares.T, axis=0, keepdims=True)
        pltpu.make_async_copy(ostage.at[pl.ds(row, C)], out_hbm.at[pl.ds(row, C)], out_sem.at[c]).start()
        return carry

    lax.fori_loop(0, chunks, carried_step, 0)

    third = []
    for step in range(1, heads):
        peer = lax.rem(my_head + step, heads)
        third.append(remote(sq, sqgot.at[step - 1], s3.at[step - 1], r3.at[step - 1], {"head": peer}))
        third[-1].start()
    for copy in halos + window_halos + first + second:
        copy.wait_send()

    def out_wait(c, carry):
        row = pl.multiple_of(c * C, C)
        pltpu.make_async_copy(ostage.at[pl.ds(row, C)], out_hbm.at[pl.ds(row, C)], out_sem.at[c]).wait()
        return carry

    lax.fori_loop(0, chunks, out_wait, 0)
    total = sq[...]
    for step, copy in enumerate(third):
        copy.wait_recv()
        total = total + sqgot[step]
    total_ref[...] = total
    for copy in third:
        copy.wait_send()


def per_device(seqs, heads, lin_qk, lin_v, conv_qk, conv_v, swa_qkv, head_gain):
    tokens = lin_qk.shape[0]
    width = lin_v.shape[1]
    local = width // DV
    chunks = tokens // C
    part = local * ROWS // seqs
    hbm = pl.BlockSpec(memory_space=pltpu.HBM)
    vmem = pl.BlockSpec(memory_space=pltpu.VMEM)
    dma = pltpu.SemaphoreType.DMA
    halos = 1 + 3 * local
    combined, squares = pl.pallas_call(
        functools.partial(kernel, seqs, heads),
        out_shape=(
            jax.ShapeDtypeStruct((tokens, width), F32),
            jax.ShapeDtypeStruct((chunks, 1, C), F32),
        ),
        in_specs=[hbm, hbm, hbm, vmem, vmem, vmem],
        out_specs=(hbm, vmem),
        scratch_shapes=[
            pltpu.VMEM((8 + tokens, 2 * DK * local), F32),
            pltpu.VMEM((local, 8 + tokens, DV), F32),
            pltpu.VMEM((local, tokens, DV), F32),
            pltpu.VMEM((2, local, WIN + tokens, DV), F32),
            pltpu.VMEM((tokens, 2 * DK * local), F32),
            pltpu.VMEM((chunks, 2 * local, 2 * DK, C), F32),
            pltpu.VMEM((local, tokens, 2 * DV), BF16),
            pltpu.VMEM((chunks + 1, local * ROWS, DV), F32),
            pltpu.VMEM((local, tokens, DV), F32),
            pltpu.VMEM((local, tokens, DV), F32),
            pltpu.VMEM((tokens, width), F32),
            pltpu.VMEM((local * ROWS, DV), F32),
            pltpu.VMEM((seqs, part, DV), F32),
            pltpu.VMEM((seqs, part, DV), F32),
            pltpu.VMEM((local * ROWS, DV), F32),
            pltpu.VMEM((chunks, 1, C), F32),
            pltpu.VMEM((heads - 1, chunks, 1, C), F32),
            dma((1 + local,)),
            dma((local, 3)),
            dma((chunks,)),
            dma((halos,)),
            dma((halos,)),
            dma((seqs - 1,)),
            dma((seqs - 1,)),
            dma((seqs - 1,)),
            dma((seqs - 1,)),
            dma((heads - 1,)),
            dma((heads - 1,)),
        ],
        compiler_params=pltpu.CompilerParams(
            collective_id=0, has_side_effects=True, vmem_limit_bytes=58 * 1024 * 1024
        ),
        name="mixer",
    )(lin_qk, lin_v, jnp.transpose(swa_qkv, (1, 0, 2)), conv_qk, conv_v, head_gain[None])
    total = squares.reshape(tokens)
    return combined * lax.rsqrt(total / (heads * width) + 1e-06)[:, None]


def solution(mesh):
    placed = (
        P("seq", "head"),
        P("seq", "head"),
        P(None, "head"),
        P(None, "head"),
        P("seq", None, "head"),
        P("head"),
    )
    return jax.shard_map(
        functools.partial(per_device, mesh.shape["seq"], mesh.shape["head"]),
        mesh=mesh, in_specs=placed, out_specs=P("seq", "head"), check_vma=False,
    )
```

profile of v0, /device:TPU:1, one launch (start us, length us, event | category | flops | bytes accessed | tf_op | source)
XLA Modules:
  0.0 80.8 jit_solution(2054983536408976143)
XLA Ops:
  0.0 75.6 %mixer.1 = (f32[2048,512]{1,0:T(8,128)}, f32[16,1,128]{2,1,0:T(1,128)}) custom-call(f32[2048,128]{1,0:T(8,128)} %qk_hbm.1, f32[2048,512]{1,0:T(8,128)} %v_hbm.1, f32[3,2048,512]{2,1,0:T(8,128)} %bitcast.3, f32[3,128]{1,0:T(4,128)} %wqk_ref.1, f32[3,512]{1,0:T(4,128)} %wv_ref.1, f32[1,512]{1,0:T(1,128)} %bitcast.5), custom_call_target="tpu_custom_call" | custom-call | tf_op jit(solution)/shard_map/mixer/pallas_call | solution.py:301
  75.6 0.7 add_rsqrt_fusion
  76.3 4.5 %broadcast_multiply_fusion = f32[2048,512]{1,0:T(8,128)} fusion(f32[2048,512]{1,0:T(8,128)} %get-tuple-element.7, f32[2048]{0:T(1024)S(1)} %bitcast.4), kind=kLoop, calls=%fused_computation | loop fusion | flops 1048576 | bytes 8396800 | tf_op jit(solution)/shard_map/mul | solution.py:345
where the time goes:
time: 81.1 us; the launch traced here: 80.8 us
  Pallas kernels  75.6 us (93%)
  other arithmetic  5.25 us (6%)
    pallas_call x1, Pallas kernels, per_device(): pl.pallas_call(functools.partial(kernel, seqs, heads), out_shape=(jax.Sha...  75.6 us
    mul x1, other arithmetic, per_device(): return combined * lax.rsqrt(total / (heads * width) + 1e-06)[:, None]  4.54 us

commit v1 on v0

v1 whole, which is shorter than its diff:
```python
import functools
import math

import jax
import jax.numpy as jnp
from jax import lax
from jax.experimental import pallas as pl
from jax.experimental.pallas import tpu as pltpu
from jax.sharding import PartitionSpec as P

DK = 16
DV = 128
WIN = 64
C = 128
QUARTERS = 4
LOCAL_GROUP = 4
WINDOW_GROUP = 16
CARRIED_GROUP = 2
ROWS = 160
MESH = pl.DeviceIdType.MESH
F32 = jnp.float32
BF16 = jnp.bfloat16


def split(value):
    high = value.astype(BF16)
    low = (value - high.astype(F32)).astype(BF16)
    return high, low


def dot(left, right, dims=((1,), (0,))):
    return lax.dot_general(left, right, (dims, ((), ())), preferred_element_type=F32)


def fold(value):
    return value[:, :DV] + value[:, DV:]


def feature_rows(load, pair, linear, constant):
    base = load(0, DK)
    twice = base if pair == 1 else base * pair
    rows = [base * base]
    rows += [twice * load(shift, DK) for shift in range(1, DK // 2)]
    rows += [twice[: DK // 2] * load(DK // 2, DK // 2)]
    rows += [base if linear == 1 else base * linear]
    first = lax.broadcasted_iota(jnp.int32, (8, base.shape[1]), 0) == 0
    rows += [jnp.where(first, F32(constant), F32(0.0))]
    return jnp.concatenate(rows, axis=0)


def kernel(
    seqs, heads,
    qk_hbm, v_hbm, swa_hbm, wqk_ref, wv_ref, gain_ref,
    out_ref, total_ref,
    xin, vin, qin, kin, xs, xt, us, sx, lin, win,
    mine, got, prefs, pref, sq, sqgot,
    in_sem, swa_sem, hs_sem, hr_sem, s1, r1, s2, r2, s3, r3,
):
    tokens = xs.shape[0]
    local = vin.shape[0]
    chunks = tokens // C
    part = local * ROWS // seqs
    quarter = tokens // QUARTERS
    me = lax.axis_index("seq")
    my_head = lax.axis_index("head")

    def lin_loads(n):
        at = pl.multiple_of(n * quarter, 8)
        copies = [pltpu.make_async_copy(
            qk_hbm.at[pl.ds(at, quarter)], xin.at[pl.ds(8 + at, quarter)], in_sem.at[n, 0])]
        for h in range(local):
            copies.append(pltpu.make_async_copy(
                v_hbm.at[pl.ds(at, quarter), pl.ds(h * DV, DV)], vin.at[h, pl.ds(8 + at, quarter)],
                in_sem.at[n, 1 + h]))
        return copies

    for n in range(QUARTERS):
        for load in lin_loads(n):
            load.start()

    barrier = pltpu.get_barrier_semaphore()
    for step in range(1, seqs):
        pl.semaphore_signal(barrier, inc=1, device_id={"seq": lax.rem(me + step, seqs)}, device_id_type=MESH)
    for step in range(1, heads):
        pl.semaphore_signal(barrier, inc=1, device_id={"head": lax.rem(my_head + step, heads)}, device_id_type=MESH)

    swa_loads = []
    for h in range(local):
        columns = pl.ds(h * DV, DV)
        swa_loads.append(pltpu.make_async_copy(swa_hbm.at[0, :, columns], qin.at[h], swa_sem.at[h, 0]))
        for which in range(2):
            swa_loads.append(pltpu.make_async_copy(
                swa_hbm.at[1 + which, :, columns], kin.at[which, h, pl.ds(WIN, tokens)], swa_sem.at[h, 1 + which]))

    pl.semaphore_wait(barrier, seqs - 1 + heads - 1)
    after = {"seq": lax.rem(me + 1, seqs)}

    def remote(source, target, send, receive, device):
        return pltpu.make_async_remote_copy(
            src_ref=source, dst_ref=target, send_sem=send, recv_sem=receive, device_id=device, device_id_type=MESH)

    tail = pl.ds(tokens - 8, 8)
    halos = [remote(qk_hbm.at[tail], xin.at[pl.ds(0, 8)], hs_sem.at[0], hr_sem.at[0], after)]
    for h in range(local):
        halos.append(remote(v_hbm.at[tail, pl.ds(h * DV, DV)], vin.at[h, pl.ds(0, 8)],
                            hs_sem.at[1 + h], hr_sem.at[1 + h], after))
    window_halos = []
    for h in range(local):
        for which in range(2):
            slot = 1 + local + 2 * h + which
            window_halos.append(remote(
                swa_hbm.at[1 + which, pl.ds(tokens - WIN, WIN), pl.ds(h * DV, DV)],
                kin.at[which, h, pl.ds(0, WIN)], hs_sem.at[slot], hr_sem.at[slot], after))
    for copy in halos:
        copy.start()

    sx[0] = jnp.zeros(sx.shape[1:], F32)
    for load in lin_loads(0):
        load.wait()
    per_quarter = chunks // QUARTERS
    steps = chunks // 2

    def state_step(i, carry):
        last = i == steps - 1

        @pl.when((lax.rem(2 * i + 2, per_quarter) == 0) & jnp.logical_not(last))
        def _():
            for load in lin_loads((2 * i + 2) // per_quarter):
                load.wait()

        @pl.when(last)
        def _():
            for copy in halos:
                copy.wait_recv()
            keep = me > 0
            xin[pl.ds(0, 8)] = jnp.where(keep, xin[pl.ds(0, 8)], 0.0)
            for h in range(local):
                vin[h, pl.ds(0, 8)] = jnp.where(keep, vin[h, pl.ds(0, 8)], 0.0)

        which_chunks = (2 * i + 1, lax.rem(2 * i + 2, chunks))
        pairs = [(c, h) for c in range(2) for h in range(local)]
        turned = []
        for c in which_chunks:
            row = pl.multiple_of(c * C, C)
            x = wqk_ref[0:1] * xin[pl.ds(row + 6, C)]
            x = x + wqk_ref[1:2] * xin[pl.ds(row + 7, C)]
            x = x + wqk_ref[2:3] * xin[pl.ds(row + 8, C)]
            xs[pl.ds(row, C)] = x
            turned.append(x.T)
        boths = []
        for n, h in pairs:
            row = pl.multiple_of(which_chunks[n] * C, C)
            columns = slice(h * DV, (h + 1) * DV)
            u = wv_ref[0:1, columns] * vin[h, pl.ds(row + 6, C)]
            u = u + wv_ref[1:2, columns] * vin[h, pl.ds(row + 7, C)]
            u = u + wv_ref[2:3, columns] * vin[h, pl.ds(row + 8, C)]
            both = jnp.concatenate(split(u), axis=1)
            us[h, pl.ds(row, C)] = both
            boths.append(both)
        for c, value in zip(which_chunks, turned):
            for piece in range(2 * local):
                at = value[piece * DK:(piece + 1) * DK]
                xt[c, piece, 0:DK] = at
                xt[c, piece, DK:2 * DK] = at
        phis = []
        for n, h in pairs:
            c = which_chunks[n]
            phi = feature_rows(lambda start, size: xt[c, 2 * h + 1, start:start + size], 1, 1, 1.0)
            phis.append(jnp.concatenate(split(phi), axis=1))
        states = [dot(phi, jnp.concatenate([both, both], axis=0)) for phi, both in zip(phis, boths)]
        again = jnp.where(last, 0.0, 1.0).astype(F32)
        for h in range(local):
            rows = slice(h * ROWS, (h + 1) * ROWS)
            total = sx[2 * i, rows] + fold(states[h])
            sx[2 * i + 1, rows] = total
            sx[2 * i + 2, rows] = total * again + fold(states[local + h])
        return carry

    lax.fori_loop(0, steps, state_step, 0)

    mine[...] = sx[chunks - 1] + sx[chunks]
    first = []
    for step in range(1, seqs):
        peer = lax.rem(me + step, seqs)
        rows = pl.ds(pl.multiple_of(peer * part, 8), part)
        first.append(remote(mine.at[rows], got.at[me], s1.at[step - 1], r1.at[step - 1], {"seq": peer}))
        first[-1].start()
    got[me] = mine[pl.ds(pl.multiple_of(me * part, 8), part)]
    for copy in window_halos:
        copy.start()
    for load in swa_loads:
        load.start()

    lane = lax.broadcasted_iota(jnp.int32, (C, C), 1)
    sub = lax.broadcasted_iota(jnp.int32, (C, C), 0)
    query_lane = lax.rem(lane, 2 * DK) < DK
    causal = lane <= sub

    def local_step(i, carry):
        which_chunks = [LOCAL_GROUP * i + n for n in range(LOCAL_GROUP)]
        at_rows = [pl.ds(pl.multiple_of(c * C, C), C) for c in which_chunks]
        lefts = []
        for rows in at_rows:
            x = xs[rows]
            lefts.append(jnp.concatenate(split(jnp.where(query_lane, x, pltpu.roll(x, DK, 1))), axis=1))
        rights = []
        for c in which_chunks:
            for pair in range(local // 2):
                sides = []
                for h in (2 * pair, 2 * pair + 1):
                    high, low = split(xt[c, 2 * h + 1, 0:DK])
                    blank = jnp.zeros((DK, C), BF16)
                    pieces = [blank] * (2 * 2 * local)
                    pieces[2 * h] = high
                    pieces[2 * h + 1] = low
                    pieces[2 * local + 2 * h] = high
                    sides.append(jnp.concatenate(pieces, axis=0))
                rights.append(jnp.concatenate(sides, axis=1))
        scores = [dot(lefts[n], rights[n * (local // 2) + pair])
                  for n in range(LOCAL_GROUP) for pair in range(local // 2)]
        values = []
        for score in scores:
            for which in range(2):
                value = score[:, which * C:(which + 1) * C] + 4.0
                value = jnp.where(causal, value * value + 16.0, 0.0)
                values.append(jnp.concatenate(split(value), axis=1))
        sums = []
        for n in range(LOCAL_GROUP):
            for h in range(local):
                both = us[h, at_rows[n]]
                sums.append(dot(values[n * local + h], jnp.concatenate([both, both], axis=0)))
        for n in range(LOCAL_GROUP):
            for h in range(local):
                lin[h, at_rows[n]] = fold(sums[n * local + h])
        return carry

    lax.fori_loop(0, chunks // LOCAL_GROUP, local_step, 0)

    for copy in first:
        copy.wait_recv()

    def prefix_step(d, carry):
        prefs[d] = carry
        return carry + got[d]

    lax.fori_loop(0, seqs, prefix_step, jnp.zeros((part, DV), F32))
    own_rows = pl.ds(pl.multiple_of(me * part, 8), part)
    second = []
    for step in range(1, seqs):
        peer = lax.rem(me + step, seqs)
        second.append(remote(prefs.at[peer], pref.at[own_rows], s2.at[step - 1], r2.at[step - 1], {"seq": peer}))
        second[-1].start()
    pref[own_rows] = prefs[me]

    for load in swa_loads:
        load.wait()
    for copy in window_halos:
        copy.wait_recv()
    key = lax.broadcasted_iota(jnp.int32, (WIN, C), 1)
    query = lax.broadcasted_iota(jnp.int32, (WIN, C), 0)
    scale = math.log2(math.e) / math.sqrt(DV)
    own_half = lax.rem(lax.broadcasted_iota(jnp.int32, (C, 2 * C), 1), C) < WIN
    inside = ((key < WIN) & (key <= query)) | ((key >= WIN) & (key - C > query - WIN))
    lowest = jnp.where(me == 0, C, 0)
    starts = inside & ((key < WIN) | (key >= lowest))
    bias_first = jnp.where(starts, 0.0, -1e30).astype(F32)
    bias_even = jnp.where(inside, 0.0, -1e30).astype(F32)
    bias_odd = jnp.where((key <= query + WIN) & (key > query), 0.0, -1e30).astype(F32)

    def window_step(i, carry):
        h = i // (chunks // WINDOW_GROUP)
        g = lax.rem(i, chunks // WINDOW_GROUP)
        base = pl.multiple_of(g * (WINDOW_GROUP * C), C)

        def rows_of(which, j):
            return kin[which, h, pl.ds(base + j * WIN, WIN)]

        tiles = [jnp.concatenate(split(kin[0, h, pl.ds(base + WIN + j * C, C)].T), axis=1)
                 for j in range(WINDOW_GROUP)]
        ring = jnp.concatenate(split(jnp.concatenate([rows_of(0, 1), rows_of(0, 0)], axis=0).T), axis=1)
        opening = jnp.where(g == 0, bias_first, bias_even)
        scores = []
        for j in range(WINDOW_GROUP):
            own = tiles[j]
            if j > 0:
                ring = jnp.where(own_half, own, tiles[j - 1])
            q_both = jnp.concatenate(split(qin[h, pl.ds(base + j * C, C)] * scale), axis=1)
            scores.append(fold(dot(q_both[:WIN], jnp.concatenate([ring, ring], axis=0)))
                          + (opening if j == 0 else bias_even))
            scores.append(fold(dot(q_both[WIN:], jnp.concatenate([own, own], axis=0))) + bias_odd)
        weights = []
        for score in scores:
            weight = jnp.exp2(score - jnp.max(score, axis=1, keepdims=True))
            weights.append((jnp.concatenate(split(weight), axis=1), jnp.sum(weight, axis=1, keepdims=True)))
        values = [jnp.concatenate(split(rows_of(1, j)), axis=1) for j in range(2 * WINDOW_GROUP + 1)]
        for j, (weight, norm) in enumerate(weights):
            even = j if j % 2 else j + 1
            odd = j + 1 if j % 2 else j
            tile = [values[even], values[odd]]
            win[h, pl.ds(base + j * WIN, WIN)] = fold(dot(weight, jnp.concatenate(tile + tile, axis=0))) / norm
        return carry

    lax.fori_loop(0, local * chunks // WINDOW_GROUP, window_step, 0)

    for copy in second:
        copy.wait_recv()

    def carried_step(i, carry):
        which_chunks = [CARRIED_GROUP * i + n for n in range(CARRIED_GROUP)]
        at_rows = [pl.ds(pl.multiple_of(c * C, C), C) for c in which_chunks]
        pairs = [(n, h) for n in range(CARRIED_GROUP) for h in range(local)]
        phis = []
        for n, h in pairs:
            phi = feature_rows(
                lambda start, size: xt[which_chunks[n], 2 * h, start:start + size], 2.0, 8.0, 32.0)
            phis.append(jnp.concatenate(split(phi), axis=0).T)
        states = []
        for n, h in pairs:
            c = which_chunks[n]
            rows = slice(h * ROWS, (h + 1) * ROWS)
            later = jnp.where(c > 0, 1.0, 0.0).astype(F32)
            state = sx[jnp.maximum(c - 1, 0), rows] + (pref[rows] + sx[chunks, rows] * later)
            both = jnp.concatenate(split(state), axis=1)
            states.append(jnp.concatenate([both, both], axis=0))
        earlier = [dot(phi, state) for phi, state in zip(phis, states)]
        mixes = [lin[h, at_rows[n]] + fold(earlier[n * local + h]) for n, h in pairs]
        means = [jnp.sum(mix * mix, axis=1, keepdims=True) * (1.0 / DV) for mix in mixes]
        squares = [jnp.zeros((C, DV), F32) for _ in which_chunks]
        for (n, h), mix, mean in zip(pairs, mixes, means):
            columns = slice(h * DV, (h + 1) * DV)
            value = mix * lax.rsqrt(mean + 1024.0e-6) * gain_ref[0:1, columns] + win[h, at_rows[n]]
            out_ref[at_rows[n], columns] = value
            squares[n] = squares[n] + value * value
        for c, square in zip(which_chunks, squares):
            sq[c] = jnp.sum(square.T, axis=0, keepdims=True)
        return carry

    lax.fori_loop(0, chunks // CARRIED_GROUP, carried_step, 0)

    third = []
    for step in range(1, heads):
        peer = lax.rem(my_head + step, heads)
        third.append(remote(sq, sqgot.at[step - 1], s3.at[step - 1], r3.at[step - 1], {"head": peer}))
        third[-1].start()
    for copy in halos + window_halos + first + second:
        copy.wait_send()
    total = sq[...]
    for step, copy in enumerate(third):
        copy.wait_recv()
        total = total + sqgot[step]
    total_ref[...] = total
    for copy in third:
        copy.wait_send()


def scale_kernel(count, value_ref, total_ref, out_hbm, stage, sems):
    chunks, width = total_ref.shape[0], value_ref.shape[1]
    copies = []
    for c in range(chunks):
        rows = pl.ds(c * C, C)
        factor = lax.rsqrt(total_ref[c] * (1.0 / count) + 1e-06)
        factor = jnp.broadcast_to(factor, (C, C)).T
        for h in range(width // DV):
            columns = slice(h * DV, (h + 1) * DV)
            stage[rows, columns] = value_ref[rows, columns] * factor
        copies.append(pltpu.make_async_copy(stage.at[rows], out_hbm.at[rows], sems.at[c]))
        copies[-1].start()
    for copy in copies:
        copy.wait()


def per_device(seqs, heads, lin_qk, lin_v, conv_qk, conv_v, swa_qkv, head_gain):
    tokens = lin_qk.shape[0]
    width = lin_v.shape[1]
    local = width // DV
    chunks = tokens // C
    part = local * ROWS // seqs
    hbm = pl.BlockSpec(memory_space=pltpu.HBM)
    vmem = pl.BlockSpec(memory_space=pltpu.VMEM)
    dma = pltpu.SemaphoreType.DMA
    halos = 1 + 3 * local
    combined, squares = pl.pallas_call(
        functools.partial(kernel, seqs, heads),
        out_shape=(
            jax.ShapeDtypeStruct((tokens, width), F32),
            jax.ShapeDtypeStruct((chunks, 1, C), F32),
        ),
        in_specs=[hbm, hbm, hbm, vmem, vmem, vmem],
        out_specs=(vmem, vmem),
        scratch_shapes=[
            pltpu.VMEM((8 + tokens, 2 * DK * local), F32),
            pltpu.VMEM((local, 8 + tokens, DV), F32),
            pltpu.VMEM((local, tokens, DV), F32),
            pltpu.VMEM((2, local, WIN + tokens, DV), F32),
            pltpu.VMEM((tokens, 2 * DK * local), F32),
            pltpu.VMEM((chunks, 2 * local, 2 * DK, C), F32),
            pltpu.VMEM((local, tokens, 2 * DV), BF16),
            pltpu.VMEM((chunks + 1, local * ROWS, DV), F32),
            pltpu.VMEM((local, tokens, DV), F32),
            pltpu.VMEM((local, tokens, DV), F32),
            pltpu.VMEM((local * ROWS, DV), F32),
            pltpu.VMEM((seqs, part, DV), F32),
            pltpu.VMEM((seqs, part, DV), F32),
            pltpu.VMEM((local * ROWS, DV), F32),
            pltpu.VMEM((chunks, 1, C), F32),
            pltpu.VMEM((heads - 1, chunks, 1, C), F32),
            dma((QUARTERS, 1 + local)),
            dma((local, 3)),
            dma((halos,)),
            dma((halos,)),
            dma((seqs - 1,)),
            dma((seqs - 1,)),
            dma((seqs - 1,)),
            dma((seqs - 1,)),
            dma((heads - 1,)),
            dma((heads - 1,)),
        ],
        compiler_params=pltpu.CompilerParams(
            collective_id=0, has_side_effects=True, vmem_limit_bytes=48 * 1024 * 1024
        ),
        name="mixer",
    )(lin_qk, lin_v, jnp.transpose(swa_qkv, (1, 0, 2)), conv_qk, conv_v, head_gain[None])
    return pl.pallas_call(
        functools.partial(scale_kernel, heads * width),
        out_shape=jax.ShapeDtypeStruct((tokens, width), F32),
        in_specs=[vmem, vmem],
        out_specs=hbm,
        scratch_shapes=[pltpu.VMEM((tokens, width), F32), dma((chunks,))],
        compiler_params=pltpu.CompilerParams(vmem_limit_bytes=16 * 1024 * 1024),
        name="scale",
    )(combined, squares)


def solution(mesh):
    placed = (
        P("seq", "head"),
        P("seq", "head"),
        P(None, "head"),
        P(None, "head"),
        P("seq", None, "head"),
        P("head"),
    )
    return jax.shard_map(
        functools.partial(per_device, mesh.shape["seq"], mesh.shape["head"]),
        mesh=mesh, in_specs=placed, out_specs=P("seq", "head"), check_vma=False,
    )
```

time: 81.1 us -> 49.5 us (0.61)
  Pallas kernels: 75.6 us -> 46 us
  other arithmetic: 5.25 us -> 0 us
  local copies, waits for them, and re-layouts: 0 us -> 3.28 us
    pallas_call x1, Pallas kernels: 75.6 us -> 43.7 us  [per_device(): pl.pallas_call(functools.partial(kernel, seqs, heads), out_shape=(jax.Sha...]
    mul x1 -> x0, other arithmetic: 4.54 us -> none  [per_device(): return combined * lax.rsqrt(total / (heads * width) + 1e-06)[:, None]]
    unnamed x0 -> x8, local copies, waits for them, and re-layouts: none -> 3.28 us
    pallas_call x0 -> x1, Pallas kernels: none -> 2.25 us  [per_device(): pl.pallas_call(functools.partial(scale_kernel, heads * width), out_shape=...]
where the time goes in v1:
time: 49.5 us; the launch traced here: 49.3 us
  Pallas kernels  46 us (93%)
  local copies, waits for them, and re-layouts  3.28 us (7%)
    pallas_call x1, Pallas kernels, per_device(): pl.pallas_call(functools.partial(kernel, seqs, heads), out_shape=(jax.Sha...  43.7 us
    unnamed x8, local copies, waits for them, and re-layouts  3.28 us
    pallas_call x1, Pallas kernels, per_device(): pl.pallas_call(functools.partial(scale_kernel, heads * width), out_shape=...  2.25 us

profile of v1, /device:TPU:1, one launch (start us, length us, event | category | flops | bytes accessed | tf_op | source)
XLA Modules:
  0.0 49.3 jit_solution(12879783376003967713)
XLA Ops:
  0.0 0.0 copy-start
  0.0 1.2 %copy-done = f32[2048,128]{1,0:T(8,128)S(1)} copy-done((f32[2048,128]{1,0:T(8,128)S(1)}, f32[2048,128]{1,0:T(8,128)}, u32[]{:S(2)}) %copy-start) | copy-done | bytes 1048600
  1.2 0.0 copy-start.1
  1.2 0.7 %copy-done.1 = f32[3,512]{1,0:T(4,128)S(1)} copy-done((f32[3,512]{1,0:T(4,128)S(1)}, f32[3,512]{1,0:T(4,128)}, u32[]{:S(2)}) %copy-start.1) | copy-done | bytes 6168
  1.9 0.0 copy-start.2
  1.9 0.7 %copy-done.2 = f32[3,128]{1,0:T(4,128)S(1)} copy-done((f32[3,128]{1,0:T(4,128)S(1)}, f32[3,128]{1,0:T(4,128)}, u32[]{:S(2)}) %copy-start.2) | copy-done | bytes 1560
  2.6 0.0 copy-start.3
  2.6 0.7 %copy-done.3 = f32[512]{0:T(512)S(1)} copy-done((f32[512]{0:T(512)S(1)}, f32[512]{0:T(512)}, u32[]{:S(2)}) %copy-start.3) | copy-done | bytes 2072
  3.3 43.7 %mixer.1 = (f32[2048,512]{1,0:T(8,128)S(1)}, f32[16,1,128]{2,1,0:T(1,128)S(1)}) custom-call(f32[2048,128]{1,0:T(8,128)S(1)} %copy-done, f32[2048,512]{1,0:T(8,128)} %v_hbm.1, f32[3,2048,512]{2,1,0:T(8,128)} %bitcast.3, f32[3,128]{1,0:T(4,128)S(1)} %copy-done.2, f32[3,512]{1,0:T(4,128)S(1)} %copy-done.1, f32[1,512]{1,0:T(1,128)S(1)} %bitcast.2), custom_call_target="tpu_custom_call" | custom-call | tf_op jit(solution)/shard_map/mixer/pallas_call | solution.py:382
  47.0 2.2 %scale.1 = f32[2048,512]{1,0:T(8,128)} custom-call(f32[2048,512]{1,0:T(8,128)S(1)} %get-tuple-element.7.value_ref, f32[16,1,128]{2,1,0:T(1,128)S(1)} %get-tuple-element.8.total_ref), custom_call_target="tpu_custom_call" | custom-call | tf_op jit(solution)/shard_map/scale/pallas_call | solution.py:423
Async XLA Ops:
  0.0 1.2 %copy-start = (f32[2048,128]{1,0:T(8,128)S(1)}, f32[2048,128]{1,0:T(8,128)}, u32[]{:S(2)}) copy-start(f32[2048,128]{1,0:T(8,128)} %qk_hbm.1) | copy-start | bytes 3145732
  1.2 0.7 %copy-start.1 = (f32[3,512]{1,0:T(4,128)S(1)}, f32[3,512]{1,0:T(4,128)}, u32[]{:S(2)}) copy-start(f32[3,512]{1,0:T(4,128)} %wv_ref.1) | copy-start | bytes 18436
  1.9 0.7 %copy-start.2 = (f32[3,128]{1,0:T(4,128)S(1)}, f32[3,128]{1,0:T(4,128)}, u32[]{:S(2)}) copy-start(f32[3,128]{1,0:T(4,128)} %wqk_ref.1) | copy-start | bytes 4612
  2.6 0.7 %copy-start.3 = (f32[512]{0:T(512)S(1)}, f32[512]{0:T(512)}, u32[]{:S(2)}) copy-start(f32[512]{0:T(512)} %param.11) | copy-start | bytes 6148

commit v2 on v1

--- a/solution.py
+++ b/solution.py
@@ -15,7 +15,8 @@
 QUARTERS = 4
 LOCAL_GROUP = 4
 WINDOW_GROUP = 16
-CARRIED_GROUP = 2
+CARRIED_GROUP = 4
+PREFIX_HEAD = 1
 ROWS = 160
 MESH = pl.DeviceIdType.MESH
 F32 = jnp.float32
@@ -84,15 +85,17 @@
     for step in range(1, heads):
         pl.semaphore_signal(barrier, inc=1, device_id={"head": lax.rem(my_head + step, heads)}, device_id_type=MESH)
 
-    swa_loads = []
+    def head_loads(h):
+        columns = pl.ds(pl.multiple_of(h * DV, DV), DV)
+        copies = [pltpu.make_async_copy(swa_hbm.at[0, :, columns], qin.at[h], swa_sem.at[h, 0])]
+        for which in range(2):
+            copies.append(pltpu.make_async_copy(
+                swa_hbm.at[1 + which, :, columns], kin.at[which, h, pl.ds(WIN, tokens)], swa_sem.at[h, 1 + which]))
+        return copies
+
     for h in range(local):
-        columns = pl.ds(h * DV, DV)
-        swa_loads.append(pltpu.make_async_copy(swa_hbm.at[0, :, columns], qin.at[h], swa_sem.at[h, 0]))
-        for which in range(2):
-            swa_loads.append(pltpu.make_async_copy(
-                swa_hbm.at[1 + which, :, columns], kin.at[which, h, pl.ds(WIN, tokens)], swa_sem.at[h, 1 + which]))
-
-    pl.semaphore_wait(barrier, seqs - 1 + heads - 1)
+        for load in head_loads(h):
+            load.start()
     after = {"seq": lax.rem(me + 1, seqs)}
 
     def remote(source, target, send, receive, device):
@@ -111,8 +114,6 @@
             window_halos.append(remote(
                 swa_hbm.at[1 + which, pl.ds(tokens - WIN, WIN), pl.ds(h * DV, DV)],
                 kin.at[which, h, pl.ds(0, WIN)], hs_sem.at[slot], hr_sem.at[slot], after))
-    for copy in halos:
-        copy.start()
 
     sx[0] = jnp.zeros(sx.shape[1:], F32)
     for load in lin_loads(0):
@@ -127,6 +128,12 @@
         def _():
             for load in lin_loads((2 * i + 2) // per_quarter):
                 load.wait()
+
+        @pl.when(i == 1)
+        def _():
+            pl.semaphore_wait(barrier, seqs - 1 + heads - 1)
+            for copy in halos + window_halos:
+                copy.start()
 
         @pl.when(last)
         def _():
@@ -186,10 +193,6 @@
         first.append(remote(mine.at[rows], got.at[me], s1.at[step - 1], r1.at[step - 1], {"seq": peer}))
         first[-1].start()
     got[me] = mine[pl.ds(pl.multiple_of(me * part, 8), part)]
-    for copy in window_halos:
-        copy.start()
-    for load in swa_loads:
-        load.start()
 
     lane = lax.broadcasted_iota(jnp.int32, (C, C), 1)
     sub = lax.broadcasted_iota(jnp.int32, (C, C), 0)
@@ -236,24 +239,16 @@
 
     lax.fori_loop(0, chunks // LOCAL_GROUP, local_step, 0)
 
-    for copy in first:
-        copy.wait_recv()
-
-    def prefix_step(d, carry):
-        prefs[d] = carry
-        return carry + got[d]
-
-    lax.fori_loop(0, seqs, prefix_step, jnp.zeros((part, DV), F32))
     own_rows = pl.ds(pl.multiple_of(me * part, 8), part)
     second = []
     for step in range(1, seqs):
         peer = lax.rem(me + step, seqs)
         second.append(remote(prefs.at[peer], pref.at[own_rows], s2.at[step - 1], r2.at[step - 1], {"seq": peer}))
-        second[-1].start()
-    pref[own_rows] = prefs[me]
-
-    for load in swa_loads:
-        load.wait()
+
+    def prefix_step(d, carry):
+        prefs[d] = carry
+        return carry + got[d]
+
     for copy in window_halos:
         copy.wait_recv()
     key = lax.broadcasted_iota(jnp.int32, (WIN, C), 1)
@@ -271,6 +266,20 @@
         h = i // (chunks // WINDOW_GROUP)
         g = lax.rem(i, chunks // WINDOW_GROUP)
         base = pl.multiple_of(g * (WINDOW_GROUP * C), C)
+
+        @pl.when((h == PREFIX_HEAD) & (g == 0))
+        def _():
+            for copy in first:
+                copy.wait_recv()
+            lax.fori_loop(0, seqs, prefix_step, jnp.zeros((part, DV), F32))
+            for copy in second:
+                copy.start()
+            pref[own_rows] = prefs[me]
+
+        @pl.when(g == 0)
+        def _():
+            for load in head_loads(h):
+                load.wait()
 
         def rows_of(which, j):
             return kin[which, h, pl.ds(base + j * WIN, WIN)]
@@ -382,8 +391,8 @@
     combined, squares = pl.pallas_call(
         functools.partial(kernel, seqs, heads),
         out_shape=(
-            jax.ShapeDtypeStruct((tokens, width), F32),
-            jax.ShapeDtypeStruct((chunks, 1, C), F32),
+            pltpu.VMEM((tokens, width), F32),
+            pltpu.VMEM((chunks, 1, C), F32),
         ),
         in_specs=[hbm, hbm, hbm, vmem, vmem, vmem],
         out_specs=(vmem, vmem),
@@ -416,7 +425,7 @@
             dma((heads - 1,)),
         ],
         compiler_params=pltpu.CompilerParams(
-            collective_id=0, has_side_effects=True, vmem_limit_bytes=48 * 1024 * 1024
+            collective_id=0, has_side_effects=True, vmem_limit_bytes=54 * 1024 * 1024
         ),
         name="mixer",
     )(lin_qk, lin_v, jnp.transpose(swa_qkv, (1, 0, 2)), conv_qk, conv_v, head_gain[None])

time: 49.5 us -> 41.4 us (0.84)
  Pallas kernels: 46 us -> 41.2 us
  local copies, waits for them, and re-layouts: 3.28 us -> 0 us
    pallas_call x1, Pallas kernels: 43.7 us -> 39 us  [per_device(): pl.pallas_call(functools.partial(kernel, seqs, heads), out_shape=(pltpu.V...]
    unnamed x8 -> x0, local copies, waits for them, and re-layouts: 3.28 us -> none
where the time goes in v2:
time: 41.4 us; the launch traced here: 41.2 us
  Pallas kernels  41.2 us (100%)
    pallas_call x1, Pallas kernels, per_device(): pl.pallas_call(functools.partial(kernel, seqs, heads), out_shape=(pltpu.V...  39 us
    pallas_call x1, Pallas kernels, per_device(): pl.pallas_call(functools.partial(scale_kernel, heads * width), out_shape=...  2.25 us

profile of v2, /device:TPU:1, one launch (start us, length us, event | category | flops | bytes accessed | tf_op | source)
XLA Modules:
  0.0 41.2 jit_solution(3320758509561046331)
XLA Ops:
  0.0 39.0 %mixer.1 = (f32[2048,512]{1,0:T(8,128)S(1)}, f32[16,1,128]{2,1,0:T(1,128)S(1)}) custom-call(f32[2048,128]{1,0:T(8,128)} %qk_hbm.1, f32[2048,512]{1,0:T(8,128)} %v_hbm.1, f32[3,2048,512]{2,1,0:T(8,128)} %bitcast.2, f32[3,128]{1,0:T(4,128)} %wqk_ref.1, f32[3,512]{1,0:T(4,128)} %wv_ref.1, f32[1,512]{1,0:T(1,128)} %bitcast.3), custom_call_target="tpu_custom_call" | custom-call | tf_op jit(solution)/shard_map/mixer/pallas_call | solution.py:391
  39.0 2.2 %scale.1 = f32[2048,512]{1,0:T(8,128)} custom-call(f32[2048,512]{1,0:T(8,128)S(1)} %get-tuple-element.7.value_ref, f32[16,1,128]{2,1,0:T(1,128)S(1)} %get-tuple-element.8.total_ref), custom_call_target="tpu_custom_call" | custom-call | tf_op jit(solution)/shard_map/scale/pallas_call | solution.py:432

commit v3 on v2

--- a/solution.py
+++ b/solution.py
@@ -14,7 +14,6 @@
 C = 128
 QUARTERS = 4
 LOCAL_GROUP = 4
-WINDOW_GROUP = 16
 CARRIED_GROUP = 4
 PREFIX_HEAD = 1
 ROWS = 160
@@ -249,8 +248,6 @@
         prefs[d] = carry
         return carry + got[d]
 
-    for copy in window_halos:
-        copy.wait_recv()
     key = lax.broadcasted_iota(jnp.int32, (WIN, C), 1)
     query = lax.broadcasted_iota(jnp.int32, (WIN, C), 0)
     scale = math.log2(math.e) / math.sqrt(DV)
@@ -262,12 +259,18 @@
     bias_even = jnp.where(inside, 0.0, -1e30).astype(F32)
     bias_odd = jnp.where((key <= query + WIN) & (key > query), 0.0, -1e30).astype(F32)
 
-    def window_step(i, carry):
-        h = i // (chunks // WINDOW_GROUP)
-        g = lax.rem(i, chunks // WINDOW_GROUP)
-        base = pl.multiple_of(g * (WINDOW_GROUP * C), C)
-
-        @pl.when((h == PREFIX_HEAD) & (g == 0))
+    def split_queries(value):
+        return jnp.concatenate(split(value * scale), axis=1)
+
+    def split_values(h, j):
+        return jnp.concatenate(split(kin[1, h, pl.ds(j * WIN, WIN)]), axis=1)
+
+    def softmax(score):
+        weight = jnp.exp2(score - jnp.max(score, axis=1, keepdims=True))
+        return jnp.concatenate(split(weight), axis=1), jnp.sum(weight, axis=1, keepdims=True)
+
+    def window_step(h, carry):
+        @pl.when(h == PREFIX_HEAD)
         def _():
             for copy in first:
                 copy.wait_recv()
@@ -276,40 +279,37 @@
                 copy.start()
             pref[own_rows] = prefs[me]
 
-        @pl.when(g == 0)
-        def _():
-            for load in head_loads(h):
-                load.wait()
-
-        def rows_of(which, j):
-            return kin[which, h, pl.ds(base + j * WIN, WIN)]
-
-        tiles = [jnp.concatenate(split(kin[0, h, pl.ds(base + WIN + j * C, C)].T), axis=1)
-                 for j in range(WINDOW_GROUP)]
-        ring = jnp.concatenate(split(jnp.concatenate([rows_of(0, 1), rows_of(0, 0)], axis=0).T), axis=1)
-        opening = jnp.where(g == 0, bias_first, bias_even)
+        for load in head_loads(h):
+            load.wait()
+        tiles = [jnp.concatenate(split(kin[0, h, pl.ds(WIN + j * C, C)].T), axis=1) for j in range(chunks)]
         scores = []
-        for j in range(WINDOW_GROUP):
+        for j in range(chunks):
             own = tiles[j]
+            q_both = split_queries(qin[h, pl.ds(j * C, C)])
             if j > 0:
                 ring = jnp.where(own_half, own, tiles[j - 1])
-            q_both = jnp.concatenate(split(qin[h, pl.ds(base + j * C, C)] * scale), axis=1)
-            scores.append(fold(dot(q_both[:WIN], jnp.concatenate([ring, ring], axis=0)))
-                          + (opening if j == 0 else bias_even))
+                scores.append(fold(dot(q_both[:WIN], jnp.concatenate([ring, ring], axis=0))) + bias_even)
             scores.append(fold(dot(q_both[WIN:], jnp.concatenate([own, own], axis=0))) + bias_odd)
-        weights = []
-        for score in scores:
-            weight = jnp.exp2(score - jnp.max(score, axis=1, keepdims=True))
-            weights.append((jnp.concatenate(split(weight), axis=1), jnp.sum(weight, axis=1, keepdims=True)))
-        values = [jnp.concatenate(split(rows_of(1, j)), axis=1) for j in range(2 * WINDOW_GROUP + 1)]
-        for j, (weight, norm) in enumerate(weights):
+        weights = [softmax(score) for score in scores]
+        values = [split_values(h, j) for j in range(1, 2 * chunks + 1)]
+        for j, (weight, norm) in enumerate(weights, 1):
             even = j if j % 2 else j + 1
             odd = j + 1 if j % 2 else j
-            tile = [values[even], values[odd]]
-            win[h, pl.ds(base + j * WIN, WIN)] = fold(dot(weight, jnp.concatenate(tile + tile, axis=0))) / norm
+            tile = [values[even - 1], values[odd - 1]]
+            win[h, pl.ds(j * WIN, WIN)] = fold(dot(weight, jnp.concatenate(tile + tile, axis=0))) / norm
         return carry
 
-    lax.fori_loop(0, local * chunks // WINDOW_GROUP, window_step, 0)
+    lax.fori_loop(0, local, window_step, 0)
+
+    for copy in window_halos:
+        copy.wait_recv()
+    rings = [jnp.concatenate(split(jnp.concatenate(
+        [kin[0, h, pl.ds(WIN, WIN)], kin[0, h, pl.ds(0, WIN)]], axis=0).T), axis=1) for h in range(local)]
+    openings = [fold(dot(split_queries(qin[h, pl.ds(0, WIN)]), jnp.concatenate([ring, ring], axis=0))) + bias_first
+                for h, ring in enumerate(rings)]
+    for h, (weight, norm) in enumerate([softmax(score) for score in openings]):
+        tile = [split_values(h, 1), split_values(h, 0)]
+        win[h, pl.ds(0, WIN)] = fold(dot(weight, jnp.concatenate(tile + tile, axis=0))) / norm
 
     for copy in second:
         copy.wait_recv()

time: 41.4 us -> 41.3 us (level)
  no operation moved by 1% of the time
where the time goes in v3:
time: 41.3 us; the launch traced here: 41.2 us
  Pallas kernels  41.2 us (100%)
    pallas_call x1, Pallas kernels, per_device(): pl.pallas_call(functools.partial(kernel, seqs, heads), out_shape=(pltpu.V...  38.9 us
    pallas_call x1, Pallas kernels, per_device(): pl.pallas_call(functools.partial(scale_kernel, heads * width), out_shape=...  2.25 us

profile of v3, /device:TPU:1, one launch (start us, length us, event | category | flops | bytes accessed | tf_op | source)
XLA Modules:
  0.0 41.2 jit_solution(16589981133559404567)
XLA Ops:
  0.0 38.9 %mixer.1 = (f32[2048,512]{1,0:T(8,128)S(1)}, f32[16,1,128]{2,1,0:T(1,128)S(1)}) custom-call(f32[2048,128]{1,0:T(8,128)} %qk_hbm.1, f32[2048,512]{1,0:T(8,128)} %v_hbm.1, f32[3,2048,512]{2,1,0:T(8,128)} %bitcast.2, f32[3,128]{1,0:T(4,128)} %wqk_ref.1, f32[3,512]{1,0:T(4,128)} %wv_ref.1, f32[1,512]{1,0:T(1,128)} %bitcast.3), custom_call_target="tpu_custom_call" | custom-call | tf_op jit(solution)/shard_map/mixer/pallas_call | solution.py:391
  38.9 2.2 %scale.1 = f32[2048,512]{1,0:T(8,128)} custom-call(f32[2048,512]{1,0:T(8,128)S(1)} %get-tuple-element.7.value_ref, f32[16,1,128]{2,1,0:T(1,128)S(1)} %get-tuple-element.8.total_ref), custom_call_target="tpu_custom_call" | custom-call | tf_op jit(solution)/shard_map/scale/pallas_call | solution.py:432

commit v4 on v3

--- a/solution.py
+++ b/solution.py
@@ -15,7 +15,7 @@
 QUARTERS = 4
 LOCAL_GROUP = 4
 CARRIED_GROUP = 4
-PREFIX_HEAD = 1
+PREFIX_HEAD = 0
 ROWS = 160
 MESH = pl.DeviceIdType.MESH
 F32 = jnp.float32
@@ -114,6 +114,9 @@
                 swa_hbm.at[1 + which, pl.ds(tokens - WIN, WIN), pl.ds(h * DV, DV)],
                 kin.at[which, h, pl.ds(0, WIN)], hs_sem.at[slot], hr_sem.at[slot], after))
 
+    pl.semaphore_wait(barrier, seqs - 1 + heads - 1)
+    for copy in halos + window_halos[::2]:
+        copy.start()
     sx[0] = jnp.zeros(sx.shape[1:], F32)
     for load in lin_loads(0):
         load.wait()
@@ -127,12 +130,6 @@
         def _():
             for load in lin_loads((2 * i + 2) // per_quarter):
                 load.wait()
-
-        @pl.when(i == 1)
-        def _():
-            pl.semaphore_wait(barrier, seqs - 1 + heads - 1)
-            for copy in halos + window_halos:
-                copy.start()
 
         @pl.when(last)
         def _():
@@ -278,6 +275,8 @@
             for copy in second:
                 copy.start()
             pref[own_rows] = prefs[me]
+            for copy in window_halos[1::2]:
+                copy.start()
 
         for load in head_loads(h):
             load.wait()
@@ -301,21 +300,28 @@
 
     lax.fori_loop(0, local, window_step, 0)
 
-    for copy in window_halos:
-        copy.wait_recv()
-    rings = [jnp.concatenate(split(jnp.concatenate(
-        [kin[0, h, pl.ds(WIN, WIN)], kin[0, h, pl.ds(0, WIN)]], axis=0).T), axis=1) for h in range(local)]
-    openings = [fold(dot(split_queries(qin[h, pl.ds(0, WIN)]), jnp.concatenate([ring, ring], axis=0))) + bias_first
-                for h, ring in enumerate(rings)]
-    for h, (weight, norm) in enumerate([softmax(score) for score in openings]):
-        tile = [split_values(h, 1), split_values(h, 0)]
-        win[h, pl.ds(0, WIN)] = fold(dot(weight, jnp.concatenate(tile + tile, axis=0))) / norm
+    def opening_step():
+        for copy in window_halos:
+            copy.wait_recv()
+        rings = [jnp.concatenate(split(jnp.concatenate(
+            [kin[0, h, pl.ds(WIN, WIN)], kin[0, h, pl.ds(0, WIN)]], axis=0).T), axis=1) for h in range(local)]
+        openings = [fold(dot(split_queries(qin[h, pl.ds(0, WIN)]), jnp.concatenate([ring, ring], axis=0))) + bias_first
+                    for h, ring in enumerate(rings)]
+        for h, (weight, norm) in enumerate([softmax(score) for score in openings]):
+            tile = [split_values(h, 1), split_values(h, 0)]
+            win[h, pl.ds(0, WIN)] = fold(dot(weight, jnp.concatenate(tile + tile, axis=0))) / norm
 
     for copy in second:
         copy.wait_recv()
 
     def carried_step(i, carry):
-        which_chunks = [CARRIED_GROUP * i + n for n in range(CARRIED_GROUP)]
+        group = chunks // CARRIED_GROUP - 1 - i
+        which_chunks = [CARRIED_GROUP * group + n for n in range(CARRIED_GROUP)]
+
+        @pl.when(group == 0)
+        def _():
+            opening_step()
+
         at_rows = [pl.ds(pl.multiple_of(c * C, C), C) for c in which_chunks]
         pairs = [(n, h) for n in range(CARRIED_GROUP) for h in range(local)]
         phis = []

time: 41.3 us -> 39.7 us (0.961)
  Pallas kernels: 41.2 us -> 39.6 us
    pallas_call x1, Pallas kernels: 38.9 us -> 37.3 us  [per_device(): pl.pallas_call(functools.partial(kernel, seqs, heads), out_shape=(pltpu.V...]
where the time goes in v4:
time: 39.7 us; the launch traced here: 39.6 us
  Pallas kernels  39.6 us (100%)
    pallas_call x1, Pallas kernels, per_device(): pl.pallas_call(functools.partial(kernel, seqs, heads), out_shape=(pltpu.V...  37.3 us
    pallas_call x1, Pallas kernels, per_device(): pl.pallas_call(functools.partial(scale_kernel, heads * width), out_shape=...  2.25 us

profile of v4, /device:TPU:1, one launch (start us, length us, event | category | flops | bytes accessed | tf_op | source)
XLA Modules:
  0.0 39.6 jit_solution(1943849789500946245)
XLA Ops:
  0.0 37.3 %mixer.1 = (f32[2048,512]{1,0:T(8,128)S(1)}, f32[16,1,128]{2,1,0:T(1,128)S(1)}) custom-call(f32[2048,128]{1,0:T(8,128)} %qk_hbm.1, f32[2048,512]{1,0:T(8,128)} %v_hbm.1, f32[3,2048,512]{2,1,0:T(8,128)} %bitcast.2, f32[3,128]{1,0:T(4,128)} %wqk_ref.1, f32[3,512]{1,0:T(4,128)} %wv_ref.1, f32[1,512]{1,0:T(1,128)} %bitcast.3), custom_call_target="tpu_custom_call" | custom-call | tf_op jit(solution)/shard_map/mixer/pallas_call | solution.py:397
  37.3 2.2 %scale.1 = f32[2048,512]{1,0:T(8,128)} custom-call(f32[2048,512]{1,0:T(8,128)S(1)} %get-tuple-element.7.value_ref, f32[16,1,128]{2,1,0:T(1,128)S(1)} %get-tuple-element.8.total_ref), custom_call_target="tpu_custom_call" | custom-call | tf_op jit(solution)/shard_map/scale/pallas_call | solution.py:438

commit v5 on v4

--- a/solution.py
+++ b/solution.py
@@ -46,6 +46,12 @@
     first = lax.broadcasted_iota(jnp.int32, (8, base.shape[1]), 0) == 0
     rows += [jnp.where(first, F32(constant), F32(0.0))]
     return jnp.concatenate(rows, axis=0)
+
+
+def far_first(seqs):
+    side = math.isqrt(seqs)
+    return sorted(range(1, seqs), key=lambda step: -sum(
+        min(at, side - at) for at in (step // side, step % side)))
 
 
 def kernel(
@@ -183,7 +189,7 @@
 
     mine[...] = sx[chunks - 1] + sx[chunks]
     first = []
-    for step in range(1, seqs):
+    for step in far_first(seqs):
         peer = lax.rem(me + step, seqs)
         rows = pl.ds(pl.multiple_of(peer * part, 8), part)
         first.append(remote(mine.at[rows], got.at[me], s1.at[step - 1], r1.at[step - 1], {"seq": peer}))
@@ -237,7 +243,7 @@
 
     own_rows = pl.ds(pl.multiple_of(me * part, 8), part)
     second = []
-    for step in range(1, seqs):
+    for step in far_first(seqs):
         peer = lax.rem(me + step, seqs)
         second.append(remote(prefs.at[peer], pref.at[own_rows], s2.at[step - 1], r2.at[step - 1], {"seq": peer}))
 

time: 39.7 us -> 38.5 us (0.970)
  Pallas kernels: 39.6 us -> 38.3 us
    pallas_call x1, Pallas kernels: 37.3 us -> 36.1 us  [per_device(): pl.pallas_call(functools.partial(kernel, seqs, heads), out_shape=(pltpu.V...]
where the time goes in v5:
time: 38.5 us; the launch traced here: 38.3 us
  Pallas kernels  38.3 us (99%)
    pallas_call x1, Pallas kernels, per_device(): pl.pallas_call(functools.partial(kernel, seqs, heads), out_shape=(pltpu.V...  36.1 us
    pallas_call x1, Pallas kernels, per_device(): pl.pallas_call(functools.partial(scale_kernel, heads * width), out_shape=...  2.25 us

profile of v5, /device:TPU:1, one launch (start us, length us, event | category | flops | bytes accessed | tf_op | source)
XLA Modules:
  0.0 38.3 jit_solution(10143684206099881183)
XLA Ops:
  0.0 36.1 %mixer.1 = (f32[2048,512]{1,0:T(8,128)S(1)}, f32[16,1,128]{2,1,0:T(1,128)S(1)}) custom-call(f32[2048,128]{1,0:T(8,128)} %qk_hbm.1, f32[2048,512]{1,0:T(8,128)} %v_hbm.1, f32[3,2048,512]{2,1,0:T(8,128)} %bitcast.2, f32[3,128]{1,0:T(4,128)} %wqk_ref.1, f32[3,512]{1,0:T(4,128)} %wv_ref.1, f32[1,512]{1,0:T(1,128)} %bitcast.3), custom_call_target="tpu_custom_call" | custom-call | tf_op jit(solution)/shard_map/mixer/pallas_call | solution.py:403
  36.1 2.2 %scale.1 = f32[2048,512]{1,0:T(8,128)} custom-call(f32[2048,512]{1,0:T(8,128)S(1)} %get-tuple-element.7.value_ref, f32[16,1,128]{2,1,0:T(1,128)S(1)} %get-tuple-element.8.total_ref), custom_call_target="tpu_custom_call" | custom-call | tf_op jit(solution)/shard_map/scale/pallas_call | solution.py:444

commit v6 on v5

--- a/solution.py
+++ b/solution.py
@@ -15,7 +15,7 @@
 QUARTERS = 4
 LOCAL_GROUP = 4
 CARRIED_GROUP = 4
-PREFIX_HEAD = 0
+PREFIX_HEAD = 1
 ROWS = 160
 MESH = pl.DeviceIdType.MESH
 F32 = jnp.float32

time: 38.5 us -> 38.3 us (level)
  no operation moved by 1% of the time
where the time goes in v6:
time: 38.3 us; the launch traced here: 38.1 us
  Pallas kernels  38.1 us (99%)
    pallas_call x1, Pallas kernels, per_device(): pl.pallas_call(functools.partial(kernel, seqs, heads), out_shape=(pltpu.V...  35.9 us
    pallas_call x1, Pallas kernels, per_device(): pl.pallas_call(functools.partial(scale_kernel, heads * width), out_shape=...  2.25 us

profile of v6, /device:TPU:1, one launch (start us, length us, event | category | flops | bytes accessed | tf_op | source)
XLA Modules:
  0.0 38.1 jit_solution(17495730908192219884)
XLA Ops:
  0.0 35.9 %mixer.1 = (f32[2048,512]{1,0:T(8,128)S(1)}, f32[16,1,128]{2,1,0:T(1,128)S(1)}) custom-call(f32[2048,128]{1,0:T(8,128)} %qk_hbm.1, f32[2048,512]{1,0:T(8,128)} %v_hbm.1, f32[3,2048,512]{2,1,0:T(8,128)} %bitcast.2, f32[3,128]{1,0:T(4,128)} %wqk_ref.1, f32[3,512]{1,0:T(4,128)} %wv_ref.1, f32[1,512]{1,0:T(1,128)} %bitcast.3), custom_call_target="tpu_custom_call" | custom-call | tf_op jit(solution)/shard_map/mixer/pallas_call | solution.py:403
  35.9 2.2 %scale.1 = f32[2048,512]{1,0:T(8,128)} custom-call(f32[2048,512]{1,0:T(8,128)S(1)} %get-tuple-element.7.value_ref, f32[16,1,128]{2,1,0:T(1,128)S(1)} %get-tuple-element.8.total_ref), custom_call_target="tpu_custom_call" | custom-call | tf_op jit(solution)/shard_map/scale/pallas_call | solution.py:444
